TPU v7x, 512 devices: a whole 4x8x8 slice. The times are simulated.
512 devices in a mesh: row: 32 (over y, x), col: 16 (over z, core).
Axes of the slice: x: 4, y: 8, z: 8, core: 2. Of those that a mesh axis runs over, the one named last changes fastest.
Arguments:
- activations: bfloat16 [576, 8192], P('row', 'col'), may hold values from -6 to 6
- gate_matrix: bfloat16 [8192, 28672], P('col', 'row'), may hold values from -0.0625 to 0.0625
- up_matrix: bfloat16 [8192, 28672], P('col', 'row'), may hold values from -0.0625 to 0.0625
- down_matrix: bfloat16 [28672, 8192], P('row', 'col'), may hold values from -0.03125 to 0.03125
Outputs:
- layer_out: bfloat16 [576, 8192], P('row', 'col')
All inputs are finite; a program needn't handle non-finite values.
Results may differ from a plain program's by a relative error of at most 0.0049.
Values may be sent and summed in bfloat16 or wider, within the bound.
No kernel may reach another device: no remote copies, remote signals or barrier semaphores. Data moves between devices by JAX's collectives and lax.ppermute only.
A program may use at most 64 MiB of HBM per device.

v0:
```python
import jax
import jax.numpy as jnp
from jax import lax
from jax.sharding import PartitionSpec as P


def activate(summed, hidden_width):
    gate_part = summed[:, :hidden_width]
    up_part = summed[:, hidden_width:]
    return (jax.nn.silu(gate_part) * up_part).astype(jnp.bfloat16)


def shards(activations, gate_matrix, up_matrix, down_matrix):
    gathered = lax.all_gather(activations, "row", axis=0, tiled=True)
    hidden_width = gate_matrix.shape[1]
    gate_term = jnp.dot(gathered, gate_matrix, preferred_element_type=jnp.float32)
    up_term = jnp.dot(gathered, up_matrix, preferred_element_type=jnp.float32)
    summed = lax.psum(jnp.concatenate([gate_term, up_term], axis=1), "col")
    hidden = activate(summed, hidden_width)
    partial_out = jnp.dot(hidden, down_matrix, preferred_element_type=jnp.float32)
    result = lax.psum_scatter(partial_out, "row", scatter_dimension=0, tiled=True)
    return result.astype(jnp.bfloat16)


def solution(mesh):
    placed = (P("row", "col"), P("col", "row"), P("col", "row"), P("row", "col"))
    return jax.shard_map(
        shards, mesh=mesh, in_specs=placed, out_specs=P("row", "col"), check_vma=False
    )
```

profile of v0, /device:TPU:14, one launch (start us, length us, event | category | flops | bytes accessed | tf_op | source)
XLA Modules:
  0.0 315.8 jit_solution(8600206868353178816)
XLA Ops:
  6.5 0.0 copy-start
  6.5 0.0 all-reduce.4.cloned.1.call-start
  6.5 50.4 %all-gather = bf16[32,18,512]{2,1,0:T(8,128)(2,1)S(1)} all-gather(bf16[1,18,512]{2,1,0:T(8,128)(2,1)} %bitcast.9), channel_id=1, replica_groups=mesh['row'=32,'col'=16] {'row'}, dimensions={0}, use_global_device_ids=true | all-gather | bytes 608256 | tf_op jit(solution)/shard_map/all_gather | solution.py:14
  57.0 0.2 reshape.1
  57.2 0.0 copy-start.1
  57.2 0.8 fusion.6
  58.0 0.4 copy-done.1
  58.4 0.8 fusion.7
  59.1 2.3 pad_maximum_fusion
  61.4 0.0 all-reduce.4.cloned.1.call-update
  61.4 129.4 %all-reduce.4.cloned.1.call-done = f32[576,1792]{1,0:T(8,128)} async-done(((f32[576,1792]{1,0:T(8,128)}), f32[576,1792]{1,0:T(8,128)}) %all-reduce.4.cloned.1.call-update) | async-done | bytes 4128784 | tf_op jit(solution)/shard_map/psum | solution.py:18
  190.8 3.0 fusion.2
  193.8 72.6 %fusion = f32[24,512]{1,0:T(8,128)S(1)} fusion(f32[576,512]{1,0:T(8,128)S(1)} %fusion.2), kind=kCustom, calls=%all-reduce-scatter | all-reduce-scatter fusion | flops 393217 | bytes 1230848
  266.4 4.2 %collective-permute-start = (bf16[24,512]{1,0:T(8,128)(2,1)S(1)}, bf16[24,512]{1,0:T(8,128)(2,1)S(1)}, u32[]{:S(2)}, u32[]{:S(2)}) collective-permute-start(bf16[24,512]{1,0:T(8,128)(2,1)S(1)} %convert.14), channel_id=1, source_target_pairs={{0,16},{16,32},{32,48},{48,64},{64,80},{80,96},{96,112},{112,128},... | collective-permute-start | bytes 73736
  270.6 5.0 %collective-permute-start.1 = (bf16[24,512]{1,0:T(8,128)(2,1)S(1)}, bf16[24,512]{1,0:T(8,128)(2,1)S(1)}, u32[]{:S(2)}, u32[]{:S(2)}) collective-permute-start(bf16[24,512]{1,0:T(8,128)(2,1)S(1)} %convert.14), channel_id=1, source_target_pairs={{0,32},{16,48},{32,64},{48,80},{64,96},{80,112},{96,128},{112,144}... | collective-permute-start | bytes 73736
  275.6 12.3 %collective-permute-start.7 = (bf16[18,512]{1,0:T(8,128)(2,1)S(1)}, bf16[18,512]{1,0:T(8,128)(2,1)S(1)}, u32[]{:S(2)}, u32[]{:S(2)}) collective-permute-start(bf16[18,512]{1,0:T(8,128)(2,1)S(1)} %slice.10), channel_id=1, source_target_pairs={{0,128},{16,144},{32,160},{48,176},{64,192},{80,208},{96,224},{112... | collective-permute-start | bytes 55304
  287.9 1.9 collective-permute-start.2
  289.8 3.1 collective-permute-start.3
  292.9 0.0 collective-permute-done.7
  292.9 3.4 %collective-permute-start.4 = (bf16[24,512]{1,0:T(8,128)(2,1)S(1)}, bf16[24,512]{1,0:T(8,128)(2,1)S(1)}, u32[]{:S(2)}, u32[]{:S(2)}) collective-permute-start(bf16[24,512]{1,0:T(8,128)(2,1)S(1)} %convert.14), channel_id=1, source_target_pairs={{0,80},{16,96},{32,112},{48,128},{64,144},{80,160},{96,176},{112,1... | collective-permute-start | bytes 73736
  296.3 0.0 collective-permute-done
  296.3 3.0 collective-permute-start.5
  299.4 0.0 collective-permute-done.1
  299.4 1.9 collective-permute-start.6
  301.3 1.3 dynamic-slice.4
  303.2 0.0 collective-permute-done.2
  303.2 0.0 collective-permute-done.3
  303.2 0.0 collective-permute-done.4
  303.3 1.2 collective-permute-done.5
  304.5 2.8 collective-permute-done.6
  307.2 1.1 concatenate.4
  308.3 0.6 dynamic-slice_convert_fusion
  (5 shorter events, 0.0 us)
Async XLA Ops:
  6.5 50.6 %copy-start = (bf16[512,896]{1,0:T(8,128)(2,1)S(1)}, bf16[512,896]{1,0:T(8,128)(2,1)}, u32[]{:S(2)}) copy-start(bf16[512,896]{1,0:T(8,128)(2,1)} %param.5) | copy-start | bytes 2752516
  6.5 184.2 %all-reduce.4.cloned.1.call-start = ((), (), s32[]{:S(2)}) async-start(), calls=%async_computation | async-start | bytes 8257536 | tf_op jit(solution)/shard_map/psum | solution.py:18
  57.2 1.2 copy-start.1
  61.4 129.4 %copy-start.2 = (bf16[896,512]{1,0:T(8,128)(2,1)S(1)}, bf16[896,512]{1,0:T(8,128)(2,1)}, u32[]{:S(2)}) copy-start(bf16[896,512]{1,0:T(8,128)(2,1)} %param.7) | copy-start | bytes 2752516
  266.4 29.9 %collective-permute-start = (bf16[24,512]{1,0:T(8,128)(2,1)S(1)}, bf16[24,512]{1,0:T(8,128)(2,1)S(1)}, u32[]{:S(2)}, u32[]{:S(2)}) collective-permute-start(bf16[24,512]{1,0:T(8,128)(2,1)S(1)} %convert.14), channel_id=1, source_target_pairs={{0,16},{16,32},{32,48},{48,64},{64,80},{80,96},{96,112},{112,128},... | collective-permute-start | bytes 73736
  270.6 28.8 %collective-permute-start.1 = (bf16[24,512]{1,0:T(8,128)(2,1)S(1)}, bf16[24,512]{1,0:T(8,128)(2,1)S(1)}, u32[]{:S(2)}, u32[]{:S(2)}) collective-permute-start(bf16[24,512]{1,0:T(8,128)(2,1)S(1)} %convert.14), channel_id=1, source_target_pairs={{0,32},{16,48},{32,64},{48,80},{64,96},{80,112},{96,128},{112,144}... | collective-permute-start | bytes 73736
  275.6 17.3 %collective-permute-start.7 = (bf16[18,512]{1,0:T(8,128)(2,1)S(1)}, bf16[18,512]{1,0:T(8,128)(2,1)S(1)}, u32[]{:S(2)}, u32[]{:S(2)}) collective-permute-start(bf16[18,512]{1,0:T(8,128)(2,1)S(1)} %slice.10), channel_id=1, source_target_pairs={{0,128},{16,144},{32,160},{48,176},{64,192},{80,208},{96,224},{112... | collective-permute-start | bytes 55304
  287.9 15.4 %collective-permute-start.2 = (bf16[24,512]{1,0:T(8,128)(2,1)S(1)}, bf16[24,512]{1,0:T(8,128)(2,1)S(1)}, u32[]{:S(2)}, u32[]{:S(2)}) collective-permute-start(bf16[24,512]{1,0:T(8,128)(2,1)S(1)} %convert.14), channel_id=1, source_target_pairs={{0,48},{16,64},{32,80},{48,96},{64,112},{80,128},{96,144},{112,160... | collective-permute-start | bytes 73736
  289.8 13.5 %collective-permute-start.3 = (bf16[24,512]{1,0:T(8,128)(2,1)S(1)}, bf16[24,512]{1,0:T(8,128)(2,1)S(1)}, u32[]{:S(2)}, u32[]{:S(2)}) collective-permute-start(bf16[24,512]{1,0:T(8,128)(2,1)S(1)} %convert.14), channel_id=1, source_target_pairs={{0,64},{16,80},{32,96},{48,112},{64,128},{80,144},{96,160},{112,17... | collective-permute-start | bytes 73736
  292.9 10.4 %collective-permute-start.4 = (bf16[24,512]{1,0:T(8,128)(2,1)S(1)}, bf16[24,512]{1,0:T(8,128)(2,1)S(1)}, u32[]{:S(2)}, u32[]{:S(2)}) collective-permute-start(bf16[24,512]{1,0:T(8,128)(2,1)S(1)} %convert.14), channel_id=1, source_target_pairs={{0,80},{16,96},{32,112},{48,128},{64,144},{80,160},{96,176},{112,1... | collective-permute-start | bytes 73736
  296.3 8.1 %collective-permute-start.5 = (bf16[24,512]{1,0:T(8,128)(2,1)S(1)}, bf16[24,512]{1,0:T(8,128)(2,1)S(1)}, u32[]{:S(2)}, u32[]{:S(2)}) collective-permute-start(bf16[24,512]{1,0:T(8,128)(2,1)S(1)} %convert.14), channel_id=1, source_target_pairs={{0,96},{16,112},{32,128},{48,144},{64,160},{80,176},{96,192},{112,... | collective-permute-start | bytes 73736
  299.4 7.8 %collective-permute-start.6 = (bf16[24,512]{1,0:T(8,128)(2,1)S(1)}, bf16[24,512]{1,0:T(8,128)(2,1)S(1)}, u32[]{:S(2)}, u32[]{:S(2)}) collective-permute-start(bf16[24,512]{1,0:T(8,128)(2,1)S(1)} %convert.14), channel_id=1, source_target_pairs={{0,112},{16,128},{32,144},{48,160},{64,176},{80,192},{96,208},{112... | collective-permute-start | bytes 73736
Sparse Core Ops, SparseCore 0:
  61.5 129.1 all-reduce.3
where the time goes:
time: 316 us
  waiting for transfers between devices  133 us (42%)
  blocking collectives  123 us (39%)
  starting transfers between devices  34.8 us (11%)
  between operations  14.2 us (4%)
  matrix products  4.54 us (1%)
  local copies, waits for them, and re-layouts  3.62 us (1%)
    psum x1, waiting for transfers between devices, shards(): summed = lax.psum(jnp.concatenate([gate_term, up_term], axis=1), 'col')  129 us
    unnamed x1, blocking collectives  72.6 us
    all_gather x1, blocking collectives, shards(): gathered = lax.all_gather(activations, 'row', axis=0, tiled=True)  50.4 us
    unnamed x8, starting transfers between devices  34.8 us
  transfers between devices with their start and end apart: 9, of which 3 were waited for; matrix products, arithmetic and copies ran while one was open for 0% of the time, Pallas kernels for 0%

commit v1 on v0

--- a/solution.py
+++ b/solution.py
@@ -11,7 +11,9 @@
 
 
 def shards(activations, gate_matrix, up_matrix, down_matrix):
-    gathered = lax.all_gather(activations, "row", axis=0, tiled=True)
+    gathered = jnp.concatenate(
+        lax.all_to_all(jnp.stack([activations] * lax.axis_size("row")), "row", 0, 0), axis=0
+    )
     hidden_width = gate_matrix.shape[1]
     gate_term = jnp.dot(gathered, gate_matrix, preferred_element_type=jnp.float32)
     up_term = jnp.dot(gathered, up_matrix, preferred_element_type=jnp.float32)

time: 316 us -> 297 us (0.940)
  blocking collectives: 123 us -> 104 us
    all_gather x1 -> x0, blocking collectives: 50.4 us -> none  [shards(): gathered = lax.all_gather(activations, 'row', axis=0, tiled=True)]
    all_to_all x0 -> x1, blocking collectives: none -> 31.5 us  [shards(): lax.all_to_all(jnp.stack([activations] * lax.axis_size('row')), 'row', 0, 0)]
where the time goes in v1:
time: 297 us
  waiting for transfers between devices  132 us (44%)
  blocking collectives  104 us (35%)
  starting transfers between devices  34.9 us (12%)
  between operations  14.2 us (5%)
  matrix products  4.54 us (2%)
  local copies, waits for them, and re-layouts  4.49 us (2%)
    psum x1, waiting for transfers between devices, shards(): summed = lax.psum(jnp.concatenate([gate_term, up_term], axis=1), 'col')  128 us
    unnamed x1, blocking collectives  72.5 us
    unnamed x8, starting transfers between devices  34.9 us
    all_to_all x1, blocking collectives, shards(): lax.all_to_all(jnp.stack([activations] * lax.axis_size('row')), 'row', 0, 0)  31.5 us
  transfers between devices with their start and end apart: 9, of which 3 were waited for; matrix products, arithmetic and copies ran while one was open for 0% of the time, Pallas kernels for 0%

profile of v1, /device:TPU:14, one launch (start us, length us, event | category | flops | bytes accessed | tf_op | source)
XLA Modules:
  0.0 296.8 jit_solution(8170650973556186119)
XLA Ops:
  6.5 0.0 all-reduce.4.cloned.1.call-start
  6.5 0.9 stack.2
  7.4 31.5 %all_to_all.5 = bf16[32,18,512]{2,1,0:T(8,128)(2,1)S(1)} all-to-all(bf16[32,18,512]{2,1,0:T(8,128)(2,1)S(1)} %stack.2), channel_id=1, replica_groups=mesh['row'=32,'col'=16] {'row'}, dimensions={0} | all-to-all | bytes 1179648 | tf_op jit(solution)/shard_map/all_to_all | solution.py:15
  38.9 0.2 reshape.5
  39.1 0.0 copy-start.1
  39.1 0.8 fusion.6
  39.9 0.4 copy-done.1
  40.2 0.8 fusion.7
  41.0 2.3 pad_maximum_fusion
  43.3 0.0 all-reduce.4.cloned.1.call-update
  43.3 128.4 %all-reduce.4.cloned.1.call-done = f32[576,1792]{1,0:T(8,128)} async-done(((f32[576,1792]{1,0:T(8,128)}), f32[576,1792]{1,0:T(8,128)}) %all-reduce.4.cloned.1.call-update) | async-done | bytes 4128784 | tf_op jit(solution)/shard_map/psum | solution.py:20
  171.7 3.0 %fusion.2 = f32[576,512]{1,0:T(8,128)S(1)} fusion(bf16[896,512]{1,0:T(8,128)(2,1)S(1)} %copy-done.2, f32[576,1792]{1,0:T(8,128)} %all-reduce.4.cloned.1.call-done), kind=kOutput, calls=%fused_computation.3 | convolution fusion | flops 531578880 | bytes 6225920 | tf_op jit(solution)/shard_map/dot_general | solution.py:22
  174.7 72.5 %fusion = f32[24,512]{1,0:T(8,128)S(1)} fusion(f32[576,512]{1,0:T(8,128)S(1)} %fusion.2), kind=kCustom, calls=%all-reduce-scatter | all-reduce-scatter fusion | flops 393217 | bytes 1230848
  247.3 4.2 %collective-permute-start = (bf16[24,512]{1,0:T(8,128)(2,1)S(1)}, bf16[24,512]{1,0:T(8,128)(2,1)S(1)}, u32[]{:S(2)}, u32[]{:S(2)}) collective-permute-start(bf16[24,512]{1,0:T(8,128)(2,1)S(1)} %convert.14), channel_id=1, source_target_pairs={{0,16},{16,32},{32,48},{48,64},{64,80},{80,96},{96,112},{112,128},... | collective-permute-start | bytes 73736
  251.5 5.0 %collective-permute-start.1 = (bf16[24,512]{1,0:T(8,128)(2,1)S(1)}, bf16[24,512]{1,0:T(8,128)(2,1)S(1)}, u32[]{:S(2)}, u32[]{:S(2)}) collective-permute-start(bf16[24,512]{1,0:T(8,128)(2,1)S(1)} %convert.14), channel_id=1, source_target_pairs={{0,32},{16,48},{32,64},{48,80},{64,96},{80,112},{96,128},{112,144}... | collective-permute-start | bytes 73736
  256.5 12.3 %collective-permute-start.7 = (bf16[18,512]{1,0:T(8,128)(2,1)S(1)}, bf16[18,512]{1,0:T(8,128)(2,1)S(1)}, u32[]{:S(2)}, u32[]{:S(2)}) collective-permute-start(bf16[18,512]{1,0:T(8,128)(2,1)S(1)} %slice.10), channel_id=1, source_target_pairs={{0,128},{16,144},{32,160},{48,176},{64,192},{80,208},{96,224},{112... | collective-permute-start | bytes 55304
  268.8 1.9 collective-permute-start.2
  270.8 3.1 %collective-permute-start.3 = (bf16[24,512]{1,0:T(8,128)(2,1)S(1)}, bf16[24,512]{1,0:T(8,128)(2,1)S(1)}, u32[]{:S(2)}, u32[]{:S(2)}) collective-permute-start(bf16[24,512]{1,0:T(8,128)(2,1)S(1)} %convert.14), channel_id=1, source_target_pairs={{0,64},{16,80},{32,96},{48,112},{64,128},{80,144},{96,160},{112,17... | collective-permute-start | bytes 73736
  273.8 0.0 collective-permute-done.7
  273.8 3.4 %collective-permute-start.4 = (bf16[24,512]{1,0:T(8,128)(2,1)S(1)}, bf16[24,512]{1,0:T(8,128)(2,1)S(1)}, u32[]{:S(2)}, u32[]{:S(2)}) collective-permute-start(bf16[24,512]{1,0:T(8,128)(2,1)S(1)} %convert.14), channel_id=1, source_target_pairs={{0,80},{16,96},{32,112},{48,128},{64,144},{80,160},{96,176},{112,1... | collective-permute-start | bytes 73736
  277.3 0.0 collective-permute-done
  277.3 3.0 %collective-permute-start.5 = (bf16[24,512]{1,0:T(8,128)(2,1)S(1)}, bf16[24,512]{1,0:T(8,128)(2,1)S(1)}, u32[]{:S(2)}, u32[]{:S(2)}) collective-permute-start(bf16[24,512]{1,0:T(8,128)(2,1)S(1)} %convert.14), channel_id=1, source_target_pairs={{0,96},{16,112},{32,128},{48,144},{64,160},{80,176},{96,192},{112,... | collective-permute-start | bytes 73736
  280.3 0.0 collective-permute-done.1
  280.3 1.9 collective-permute-start.6
  282.3 1.3 dynamic-slice.4
  284.2 0.0 collective-permute-done.2
  284.2 0.0 collective-permute-done.3
  284.2 0.0 collective-permute-done.4
  284.2 1.2 collective-permute-done.5
  285.4 2.8 collective-permute-done.6
  288.2 1.1 concatenate.4
  289.3 0.6 dynamic-slice_convert_fusion
  (6 shorter events, 0.0 us)
Async XLA Ops:
  6.5 32.5 %copy-start = (bf16[512,896]{1,0:T(8,128)(2,1)S(1)}, bf16[512,896]{1,0:T(8,128)(2,1)}, u32[]{:S(2)}) copy-start(bf16[512,896]{1,0:T(8,128)(2,1)} %param.5) | copy-start | bytes 2752516
  6.5 165.2 %all-reduce.4.cloned.1.call-start = ((), (), s32[]{:S(2)}) async-start(), calls=%async_computation.1 | async-start | bytes 8257536 | tf_op jit(solution)/shard_map/psum | solution.py:20
  39.1 1.2 copy-start.1
  43.3 128.5 %copy-start.2 = (bf16[896,512]{1,0:T(8,128)(2,1)S(1)}, bf16[896,512]{1,0:T(8,128)(2,1)}, u32[]{:S(2)}) copy-start(bf16[896,512]{1,0:T(8,128)(2,1)} %param.7) | copy-start | bytes 2752516
  247.3 30.0 %collective-permute-start = (bf16[24,512]{1,0:T(8,128)(2,1)S(1)}, bf16[24,512]{1,0:T(8,128)(2,1)S(1)}, u32[]{:S(2)}, u32[]{:S(2)}) collective-permute-start(bf16[24,512]{1,0:T(8,128)(2,1)S(1)} %convert.14), channel_id=1, source_target_pairs={{0,16},{16,32},{32,48},{48,64},{64,80},{80,96},{96,112},{112,128},... | collective-permute-start | bytes 73736
  251.5 28.8 %collective-permute-start.1 = (bf16[24,512]{1,0:T(8,128)(2,1)S(1)}, bf16[24,512]{1,0:T(8,128)(2,1)S(1)}, u32[]{:S(2)}, u32[]{:S(2)}) collective-permute-start(bf16[24,512]{1,0:T(8,128)(2,1)S(1)} %convert.14), channel_id=1, source_target_pairs={{0,32},{16,48},{32,64},{48,80},{64,96},{80,112},{96,128},{112,144}... | collective-permute-start | bytes 73736
  256.5 17.3 %collective-permute-start.7 = (bf16[18,512]{1,0:T(8,128)(2,1)S(1)}, bf16[18,512]{1,0:T(8,128)(2,1)S(1)}, u32[]{:S(2)}, u32[]{:S(2)}) collective-permute-start(bf16[18,512]{1,0:T(8,128)(2,1)S(1)} %slice.10), channel_id=1, source_target_pairs={{0,128},{16,144},{32,160},{48,176},{64,192},{80,208},{96,224},{112... | collective-permute-start | bytes 55304
  268.8 15.4 %collective-permute-start.2 = (bf16[24,512]{1,0:T(8,128)(2,1)S(1)}, bf16[24,512]{1,0:T(8,128)(2,1)S(1)}, u32[]{:S(2)}, u32[]{:S(2)}) collective-permute-start(bf16[24,512]{1,0:T(8,128)(2,1)S(1)} %convert.14), channel_id=1, source_target_pairs={{0,48},{16,64},{32,80},{48,96},{64,112},{80,128},{96,144},{112,160... | collective-permute-start | bytes 73736
  270.8 13.5 %collective-permute-start.3 = (bf16[24,512]{1,0:T(8,128)(2,1)S(1)}, bf16[24,512]{1,0:T(8,128)(2,1)S(1)}, u32[]{:S(2)}, u32[]{:S(2)}) collective-permute-start(bf16[24,512]{1,0:T(8,128)(2,1)S(1)} %convert.14), channel_id=1, source_target_pairs={{0,64},{16,80},{32,96},{48,112},{64,128},{80,144},{96,160},{112,17... | collective-permute-start | bytes 73736
  273.8 10.4 %collective-permute-start.4 = (bf16[24,512]{1,0:T(8,128)(2,1)S(1)}, bf16[24,512]{1,0:T(8,128)(2,1)S(1)}, u32[]{:S(2)}, u32[]{:S(2)}) collective-permute-start(bf16[24,512]{1,0:T(8,128)(2,1)S(1)} %convert.14), channel_id=1, source_target_pairs={{0,80},{16,96},{32,112},{48,128},{64,144},{80,160},{96,176},{112,1... | collective-permute-start | bytes 73736
  277.3 8.1 %collective-permute-start.5 = (bf16[24,512]{1,0:T(8,128)(2,1)S(1)}, bf16[24,512]{1,0:T(8,128)(2,1)S(1)}, u32[]{:S(2)}, u32[]{:S(2)}) collective-permute-start(bf16[24,512]{1,0:T(8,128)(2,1)S(1)} %convert.14), channel_id=1, source_target_pairs={{0,96},{16,112},{32,128},{48,144},{64,160},{80,176},{96,192},{112,... | collective-permute-start | bytes 73736
  280.3 7.8 %collective-permute-start.6 = (bf16[24,512]{1,0:T(8,128)(2,1)S(1)}, bf16[24,512]{1,0:T(8,128)(2,1)S(1)}, u32[]{:S(2)}, u32[]{:S(2)}) collective-permute-start(bf16[24,512]{1,0:T(8,128)(2,1)S(1)} %convert.14), channel_id=1, source_target_pairs={{0,112},{16,128},{32,144},{48,160},{64,176},{80,192},{96,208},{112... | collective-permute-start | bytes 73736
Sparse Core Ops, SparseCore 0:
  43.4 128.2 all-reduce.3
